TPU v7x, 128 devices: a whole 4x4x4 slice. The times are simulated.
128 devices in a mesh: section: 2 (over core), dp: 8 (over y, z_lo), tensor: 8 (over z_hi, x).
Axes of the slice: x: 4, y: 4, z: 4 (z_hi: 2, z_lo: 2; z = z_hi * 2 + z_lo), core: 2. Of those that a mesh axis runs over, the one named last changes fastest.
Arguments:
- ends_in: bfloat16 [2, 16384, 1024], P('section', 'dp'), may hold values from -6 to 6
- ln_gains: float32 [2, 2, 1024], P('section'), may hold values from 0.1 to 1.9
- ln_biases: float32 [2, 2, 1024], P('section'), may hold values from -4 to 4
- qkv_weight: bfloat16 [2, 3, 1024, 1024], P('section', None, 'dp', 'tensor'), may hold values from -0.1875 to 0.1875
- qkv_bias: float32 [2, 3, 1024], P('section', None, 'tensor'), may hold values from -4 to 4
- dense_weight: bfloat16 [2, 1024, 1024], P('section', 'tensor', 'dp'), may hold values from -1.5 to 1.5
- up_weight: bfloat16 [2, 1024, 4096], P('section', 'dp', 'tensor'), may hold values from -0.1875 to 0.1875
- up_bias: float32 [2, 4096], P('section', 'tensor'), may hold values from -4 to 4
- down_weight: bfloat16 [2, 4096, 1024], P('section', 'tensor', 'dp'), may hold values from -0.09375 to 0.09375
- out_bias: float32 [2, 1024], P('section'), may hold values from -4 to 4
Outputs:
- ends_out: bfloat16 [2, 16384, 1024], P('section', 'dp')
- ln_gains_grad: float32 [2, 2, 1024], P('section')
- ln_biases_grad: float32 [2, 2, 1024], P('section')
- qkv_weight_grad: float32 [2, 3, 1024, 1024], P('section', None, 'dp', 'tensor')
- qkv_bias_grad: float32 [2, 3, 1024], P('section', None, 'tensor')
- dense_weight_grad: float32 [2, 1024, 1024], P('section', 'tensor', 'dp')
- up_weight_grad: float32 [2, 1024, 4096], P('section', 'dp', 'tensor')
- up_bias_grad: float32 [2, 4096], P('section', 'tensor')
- down_weight_grad: float32 [2, 4096, 1024], P('section', 'tensor', 'dp')
- out_bias_grad: float32 [2, 1024], P('section')
All inputs are finite; a program needn't handle non-finite values.
Results may differ from a plain program's by a relative error of at most 0.02.
Values may be sent and summed in bfloat16 or wider, within the bound.
A program may use at most 192 MiB of HBM per device.

v0:
```python
import jax
import jax.numpy as jnp
from jax import lax
from jax.sharding import PartitionSpec as P

HD = 64
LEN = 1024
MICRO = 2
ROT = 16


def passed_along(value, axis, steps):
    count = lax.axis_size(axis)
    initial, last = (max(0, -steps), min(count, count - steps))
    return lax.ppermute(value, axis, [(source, source + steps) for source in range(initial, last)])


def normalize(stream, gain_row, offset):
    center = jnp.mean(stream, axis=-1, keepdims=True)
    centred = stream - center
    inverse = lax.rsqrt(jnp.mean(centred * centred, axis=-1, keepdims=True) + 1e-05)
    scaled = centred * inverse
    return (scaled * gain_row + offset, scaled, inverse)


def norm_back(gradient, scaled, inverse, gain_row):
    weighted = gradient * gain_row
    return inverse * (
        weighted
        - jnp.mean(weighted, axis=-1, keepdims=True)
        - scaled * jnp.mean(weighted * scaled, axis=-1, keepdims=True)
    )


def rotary_tables(length):
    position = jnp.arange(length, dtype=jnp.float32)[:, None]
    exponent = jnp.arange(ROT // 2, dtype=jnp.float32) * 2.0 / ROT
    angles = position * 10000.0 ** (-exponent)
    cosine_table = jnp.concatenate([jnp.cos(angles), jnp.cos(angles)], axis=-1)[:, None, :]
    sine_table = jnp.concatenate([jnp.sin(angles), jnp.sin(angles)], axis=-1)[:, None, :]
    return (cosine_table, sine_table)


def turn(values, cosine_table, sine_table):
    rotary = values[..., :ROT]
    former = rotary[..., : ROT // 2]
    latter = rotary[..., ROT // 2 :]
    turned = jnp.concatenate([-latter, former], axis=-1)
    return jnp.concatenate(
        [rotary * cosine_table + turned * sine_table, values[..., ROT:]], axis=-1
    )


def turn_back(gradient, cosine_table, sine_table):
    rotary = gradient[..., :ROT]
    shifted = rotary * sine_table
    swapped = jnp.concatenate([shifted[..., ROT // 2 :], -shifted[..., : ROT // 2]], axis=-1)
    return jnp.concatenate([rotary * cosine_table + swapped, gradient[..., ROT:]], axis=-1)


def smooth(hidden):
    return jax.nn.gelu(hidden, approximate=False)


def block_mask(first_row, block_rows, last_row):
    return (first_row + jnp.arange(block_rows))[:, None] >= jnp.arange(last_row)[None, :]


def attend(queries, keys_all, values_all):
    length = queries.shape[1]
    block_rows = min(512, length)
    score_scale = HD ** (-0.5)
    contexts = []
    totals = []
    for first_row in range(0, length, block_rows):
        last_row = first_row + block_rows
        scores = (
            jnp.einsum(
                "sqhd,skhd->shqk",
                queries[:, first_row:last_row],
                keys_all[:, :last_row],
                preferred_element_type=jnp.float32,
            )
            * score_scale
        )
        scores = jnp.where(block_mask(first_row, block_rows, last_row), scores, -1e30)
        largest = jnp.max(scores, axis=-1, keepdims=True)
        exponent_terms = jnp.exp(scores - largest)
        summed = jnp.sum(exponent_terms, axis=-1, keepdims=True)
        weights_soft = (exponent_terms / summed).astype(jnp.bfloat16)
        contexts.append(
            jnp.einsum(
                "shqk,skhd->sqhd",
                weights_soft,
                values_all[:, :last_row],
                preferred_element_type=jnp.float32,
            )
        )
        totals.append(largest + jnp.log(summed))
    return (jnp.concatenate(contexts, axis=1), jnp.concatenate(totals, axis=2))


def attend_back(queries, keys_all, values_all, totals, d_context):
    length = queries.shape[1]
    block_rows = min(512, length)
    score_scale = HD ** (-0.5)
    d_queries = []
    d_keys = jnp.zeros(keys_all.shape, jnp.float32)
    d_values = jnp.zeros(values_all.shape, jnp.float32)
    for first_row in range(0, length, block_rows):
        last_row = first_row + block_rows
        q_block = queries[:, first_row:last_row]
        g_block = d_context[:, first_row:last_row]
        k_block = keys_all[:, :last_row]
        v_block = values_all[:, :last_row]
        scores = (
            jnp.einsum("sqhd,skhd->shqk", q_block, k_block, preferred_element_type=jnp.float32)
            * score_scale
        )
        scores = jnp.where(block_mask(first_row, block_rows, last_row), scores, -1e30)
        weights_soft = jnp.exp(scores - totals[:, :, first_row:last_row])
        d_weights = jnp.einsum(
            "sqhd,skhd->shqk", g_block, v_block, preferred_element_type=jnp.float32
        )
        d_scores = (
            weights_soft * (d_weights - jnp.sum(weights_soft * d_weights, axis=-1, keepdims=True))
        ).astype(jnp.bfloat16)
        d_queries.append(
            jnp.einsum("shqk,skhd->sqhd", d_scores, k_block, preferred_element_type=jnp.float32)
            * score_scale
        )
        d_keys = d_keys.at[:, :last_row].add(
            jnp.einsum("shqk,sqhd->skhd", d_scores, q_block, preferred_element_type=jnp.float32)
            * score_scale
        )
        d_values = d_values.at[:, :last_row].add(
            jnp.einsum(
                "shqk,sqhd->skhd",
                weights_soft.astype(jnp.bfloat16),
                g_block,
                preferred_element_type=jnp.float32,
            )
        )
    return (jnp.concatenate(d_queries, axis=1), d_keys, d_values)


def layer_forward(stream, matrices, small_params, tables):
    qkv_w, dense_w, up_w, down_w = matrices
    gain_rows, offset_rows, qkv_b, up_b, out_b = small_params
    cosine_table, sine_table = tables
    seq_count = stream.shape[0] // LEN
    local_heads = qkv_w.shape[2] // HD
    first_norm = normalize(stream, gain_rows[0], offset_rows[0])[0].astype(jnp.bfloat16)
    second_norm = normalize(stream, gain_rows[1], offset_rows[1])[0].astype(jnp.bfloat16)
    raw_proj = (
        jnp.einsum("rd,cdn->crn", first_norm, qkv_w, preferred_element_type=jnp.float32)
        + qkv_b[:, None, :]
    )
    raw_proj = raw_proj.reshape(3, seq_count, LEN, local_heads, HD)
    queries = turn(raw_proj[0], cosine_table, sine_table).astype(jnp.bfloat16)
    keys_all = turn(raw_proj[1], cosine_table, sine_table).astype(jnp.bfloat16)
    values_all = raw_proj[2].astype(jnp.bfloat16)
    context, totals = attend(queries, keys_all, values_all)
    context = context.reshape(stream.shape[0], -1).astype(jnp.bfloat16)
    hidden = jnp.dot(second_norm, up_w, preferred_element_type=jnp.float32) + up_b
    activation = smooth(hidden).astype(jnp.bfloat16)
    partial_sum = jnp.dot(context, dense_w, preferred_element_type=jnp.float32) + jnp.dot(
        activation, down_w, preferred_element_type=jnp.float32
    )
    branch = lax.psum(partial_sum.astype(jnp.bfloat16), "tensor").astype(jnp.float32)
    result = stream + branch + out_b
    return (result, (queries, keys_all, values_all, totals, context, hidden))


def layer_backward(stream, kept_state, gradient, matrices, small_params, tables):
    qkv_w, dense_w, up_w, down_w = matrices
    gain_rows, offset_rows, qkv_b, up_b, out_b = small_params
    cosine_table, sine_table = tables
    queries, keys_all, values_all, totals, context, hidden = kept_state
    token_rows = stream.shape[0]
    grad_low = gradient.astype(jnp.bfloat16)
    d_out_b = jnp.sum(gradient, axis=0)
    d_dense = jnp.einsum("rn,rd->nd", context, grad_low, preferred_element_type=jnp.float32)
    activation, smooth_pull = jax.vjp(smooth, hidden)
    d_down = jnp.einsum(
        "rf,rd->fd", activation.astype(jnp.bfloat16), grad_low, preferred_element_type=jnp.float32
    )
    d_activation = jnp.einsum("rd,fd->rf", grad_low, down_w, preferred_element_type=jnp.float32)
    d_hidden = smooth_pull(d_activation)[0].astype(jnp.bfloat16)
    d_up_b = jnp.sum(d_hidden.astype(jnp.float32), axis=0)
    second_norm, second_scaled, second_inverse = normalize(stream, gain_rows[1], offset_rows[1])
    d_up = jnp.einsum(
        "rd,rf->df", second_norm.astype(jnp.bfloat16), d_hidden, preferred_element_type=jnp.float32
    )
    d_second = jnp.einsum("rf,df->rd", d_hidden, up_w, preferred_element_type=jnp.float32)
    d_context = (
        jnp.einsum("rd,nd->rn", grad_low, dense_w, preferred_element_type=jnp.float32)
        .astype(jnp.bfloat16)
        .reshape(queries.shape)
    )
    d_queries, d_keys, d_values = attend_back(queries, keys_all, values_all, totals, d_context)
    d_raw = jnp.stack(
        [
            turn_back(d_queries, cosine_table, sine_table),
            turn_back(d_keys, cosine_table, sine_table),
            d_values,
        ]
    )
    d_raw = d_raw.reshape(3, token_rows, -1).astype(jnp.bfloat16)
    d_qkv_b = jnp.sum(d_raw.astype(jnp.float32), axis=1)
    first_norm, first_scaled, first_inverse = normalize(stream, gain_rows[0], offset_rows[0])
    d_qkv = jnp.einsum(
        "rd,crn->cdn", first_norm.astype(jnp.bfloat16), d_raw, preferred_element_type=jnp.float32
    )
    d_first = jnp.einsum("crn,cdn->rd", d_raw, qkv_w, preferred_element_type=jnp.float32)
    d_first, d_second = (
        lax.psum(d_first.astype(jnp.bfloat16), "tensor").astype(jnp.float32),
        lax.psum(d_second.astype(jnp.bfloat16), "tensor").astype(jnp.float32),
    )
    d_gains = jnp.stack(
        [jnp.sum(d_first * first_scaled, axis=0), jnp.sum(d_second * second_scaled, axis=0)]
    )
    d_offsets = jnp.stack([jnp.sum(d_first, axis=0), jnp.sum(d_second, axis=0)])
    d_stream = (
        gradient
        + norm_back(d_first, first_scaled, first_inverse, gain_rows[0])
        + norm_back(d_second, second_scaled, second_inverse, gain_rows[1])
    )
    return (
        d_stream,
        (d_qkv, d_dense, d_up, d_down),
        (d_gains, d_offsets, d_qkv_b, d_up_b, d_out_b),
    )


def fetch_each(shards):
    gathered = (
        lax.all_gather(shards[0], "dp", axis=2, tiled=True),
        lax.all_gather(shards[1], "dp", axis=2, tiled=True),
        lax.all_gather(shards[2], "dp", axis=1, tiled=True),
        lax.all_gather(shards[3], "dp", axis=2, tiled=True),
    )
    return tuple((piece[0] for piece in gathered))


def matrices_for(shards):
    return fetch_each(shards)


def body(
    ends_in,
    ln_gains,
    ln_biases,
    qkv_weight,
    qkv_bias,
    dense_weight,
    up_weight,
    up_bias,
    down_weight,
    out_bias,
):
    on_first = lax.axis_index("section") == 0
    shards = (qkv_weight, dense_weight, up_weight, down_weight)
    small_params = (ln_gains[0], ln_biases[0], qkv_bias[0], up_bias[0], out_bias[0])
    tables = rotary_tables(LEN)
    batch_rows = ends_in.shape[1] // MICRO
    zero_rows = jnp.zeros((batch_rows, ends_in.shape[2]), jnp.float32)
    inputs_kept = []
    states_kept = []
    outputs_kept = []
    arriving = zero_rows
    for micro_step in range(MICRO + 1):
        if micro_step < MICRO:
            incoming = ends_in[0, micro_step * batch_rows : (micro_step + 1) * batch_rows].astype(
                jnp.float32
            )
        else:
            incoming = zero_rows
        stream = jnp.where(on_first, incoming, arriving)
        result, kept_state = layer_forward(stream, matrices_for(shards), small_params, tables)
        inputs_kept.append(stream)
        states_kept.append(kept_state)
        outputs_kept.append(result)
        if micro_step < MICRO:
            arriving = passed_along(result.astype(jnp.bfloat16), "section", 1).astype(jnp.float32)
    weight_sums = None
    small_sums = None
    exits = []
    returning = zero_rows
    for micro_step in range(MICRO + 1):
        if micro_step < MICRO:
            outer = ends_in[1, micro_step * batch_rows : (micro_step + 1) * batch_rows].astype(
                jnp.float32
            )
        else:
            outer = zero_rows
        gradient = jnp.where(on_first, returning, outer)
        lower_index = max(micro_step - 1, 0)
        upper_index = min(micro_step + 1, MICRO)
        stream = jnp.where(on_first, inputs_kept[lower_index], inputs_kept[upper_index])
        kept_state = jax.tree.map(
            lambda before_value, after_value: jnp.where(on_first, before_value, after_value),
            states_kept[lower_index],
            states_kept[upper_index],
        )
        d_stream, d_matrices, d_smalls = layer_backward(
            stream, kept_state, gradient, matrices_for(shards), small_params, tables
        )
        if weight_sums is None:
            weight_sums = d_matrices
            small_sums = d_smalls
        else:
            weight_sums = jax.tree.map(jnp.add, weight_sums, d_matrices)
            small_sums = jax.tree.map(jnp.add, small_sums, d_smalls)
        if micro_step > 0:
            exits.append(d_stream)
        if micro_step < MICRO:
            returning = passed_along(d_stream.astype(jnp.bfloat16), "section", -1).astype(
                jnp.float32
            )
    ends_out = jnp.where(
        on_first, jnp.concatenate(exits, axis=0), jnp.concatenate(outputs_kept[1:], axis=0)
    ).astype(jnp.bfloat16)[None]
    d_qkv, d_dense, d_up, d_down = (
        lax.psum_scatter(
            weight_sums[0][None].astype(jnp.bfloat16), "dp", scatter_dimension=2, tiled=True
        ).astype(jnp.float32),
        lax.psum_scatter(
            weight_sums[1][None].astype(jnp.bfloat16), "dp", scatter_dimension=2, tiled=True
        ).astype(jnp.float32),
        lax.psum_scatter(
            weight_sums[2][None].astype(jnp.bfloat16), "dp", scatter_dimension=1, tiled=True
        ).astype(jnp.float32),
        lax.psum_scatter(
            weight_sums[3][None].astype(jnp.bfloat16), "dp", scatter_dimension=2, tiled=True
        ).astype(jnp.float32),
    )
    d_gains, d_offsets, d_qkv_b, d_up_b, d_out_b = lax.psum(
        (
            small_sums[0][None],
            small_sums[1][None],
            small_sums[2][None],
            small_sums[3][None],
            small_sums[4][None],
        ),
        "dp",
    )
    return (ends_out, d_gains, d_offsets, d_qkv, d_qkv_b, d_dense, d_up, d_up_b, d_down, d_out_b)


def solution(mesh):
    in_specs = (
        P("section", "dp", None),
        P("section", None, None),
        P("section", None, None),
        P("section", None, "dp", "tensor"),
        P("section", None, "tensor"),
        P("section", "tensor", "dp"),
        P("section", "dp", "tensor"),
        P("section", "tensor"),
        P("section", "tensor", "dp"),
        P("section", None),
    )
    out_specs = (
        P("section", "dp", None),
        P("section", None, None),
        P("section", None, None),
        P("section", None, "dp", "tensor"),
        P("section", None, "tensor"),
        P("section", "tensor", "dp"),
        P("section", "dp", "tensor"),
        P("section", "tensor"),
        P("section", "tensor", "dp"),
        P("section", None),
    )
    return jax.shard_map(body, mesh=mesh, in_specs=in_specs, out_specs=out_specs, check_vma=False)
```

profile of v0, /device:TPU:0, one launch (start us, length us, event | category | flops | bytes accessed | tf_op | source)
XLA Modules:
  0.0 1053.0 jit_solution(4330922429176152959)
XLA Ops:
  11.7 3.1 fusion.19
  17.3 34.5 %all_gather.8 = bf16[1,3,1024,128]{2,3,1,0:T(8,128)(2,1)S(1)} all-gather(bf16[1,3,128,128]{2,3,1,0:T(8,128)(2,1)S(1)} %copy.49), channel_id=1, replica_groups=mesh['section'=2,'dp'=8,'tensor'=8] {'dp'}, dimensions={2}, use_global_device_ids=true | all-gather | bytes 884736 | tf_op jit(solution)/shard_map/all_gather | solution.py:238
  51.8 3.1 fusion.126
  60.4 26.7 %all_gather.9 = bf16[1,128,1024]{2,1,0:T(8,128)(2,1)S(1)} all-gather(bf16[1,128,128]{2,1,0:T(8,128)(2,1)S(1)} %copy-done.145), channel_id=1, replica_groups=mesh['section'=2,'dp'=8,'tensor'=8] {'dp'}, dimensions={2}, use_global_device_ids=true | all-gather | bytes 294912 | tf_op jit(solution)/shard_map/all_gather | solution.py:239
  88.6 2.7 fusion.451
  91.3 3.2 fusion.123
  94.5 14.6 %all-gather.5.cloned.1.call-done = bf16[1,512,1024]{2,1,0:T(8,128)(2,1)} async-done(((bf16[1,512,128]{2,1,0:T(8,128)(2,1)}), bf16[1,512,1024]{2,1,0:T(8,128)(2,1)}) %all-gather.5.cloned.1.call-update) | async-done | bytes 1048592 | tf_op jit(solution)/shard_map/all_gather | solution.py:241
  109.2 8.5 add_convert_fusion.12
  117.7 92.8 %all-reduce.16.cloned.1.call-done = bf16[1024,1024]{1,0:T(8,128)(2,1)} async-done(((bf16[1024,1024]{1,0:T(8,128)(2,1)}), bf16[1024,1024]{1,0:T(8,128)(2,1)}) %all-reduce.16.cloned.1.call-update) | async-done | bytes 2097168 | tf_op jit(solution)/shard_map/psum | solution.py:170
  210.6 3.4 fusion.36
  215.9 3.1 collective-permute-done
  234.4 6.6 add_convert_fusion.9
  241.1 91.5 %all-reduce.18.cloned.1.call-done = bf16[1024,1024]{1,0:T(8,128)(2,1)} async-done(((bf16[1024,1024]{1,0:T(8,128)(2,1)}), bf16[1024,1024]{1,0:T(8,128)(2,1)}) %all-reduce.18.cloned.1.call-update) | async-done | bytes 2097168 | tf_op jit(solution)/shard_map/psum | solution.py:170
  332.6 3.9 fusion.90
  342.5 4.6 fusion.436
  357.2 3.1 fusion.86
  379.5 4.1 bitcast_convert_fusion.2
  383.7 13.3 %fusion.101 = (f32[1024,512]{1,0:T(8,128)}, f32[1024,512]{1,0:T(8,128)}, f32[1024,512]{1,0:T(8,128)S(1)}, f32[1024,512]{1,0:T(8,128)S(1)}, f32[1024,512]{1,0:T(8,128)}) fusion(f32[1024,512]{1,0:T(8,128)} %copy-done.219, f32[512]{0:T(512)S(1)} %bitcast.771, pred[]{:T(512)S(6)} %eq.3, f32[1024,512]{1,0:T(8,128)} %copy-done.218, ...), kind=kOutput, calls=%fused_computation.176 | convolution fusion | flops 1148715008 | bytes 17844224 | tf_op jit(solution)/shard_map/dot_general | solution.py:165
  400.5 2.6 convolution_convert_fusion.2
  404.5 107.9 %all-reduce.24.cloned.1.call-done = (bf16[1024,1024]{1,0:T(8,128)(2,1)}, bf16[1024,1024]{1,0:T(8,128)(2,1)}) async-done(((bf16[1024,1024]{1,0:T(8,128)(2,1)}, bf16[1024,1024]{1,0:T(8,128)(2,1)}), (bf16[1024,1024]{1,0:T(8,128)(2,1)}, bf16[1024,1024]{1,0:T(8,128)(2,1)})) %all-reduce.24.cloned.1.call-update) | async-done | bytes 4194320 | tf_op jit(solution)/shard_map/psum | solution.py:218
  512.4 7.6 fusion.67
  555.5 4.1 bitcast_convert_fusion.1
  559.5 4.5 convert_reduce_fusion.7
  570.3 3.9 fusion.538
  578.9 98.4 %all-reduce.22.cloned.1.call-done = (bf16[1024,1024]{1,0:T(8,128)(2,1)}, bf16[1024,1024]{1,0:T(8,128)(2,1)}) async-done(((bf16[1024,1024]{1,0:T(8,128)(2,1)}, bf16[1024,1024]{1,0:T(8,128)(2,1)}), (bf16[1024,1024]{1,0:T(8,128)(2,1)}, bf16[1024,1024]{1,0:T(8,128)(2,1)})) %all-reduce.22.cloned.1.call-update) | async-done | bytes 4194320 | tf_op jit(solution)/shard_map/psum | solution.py:217
  677.3 10.0 fusion.69
  687.4 5.3 fusion.89
  696.5 6.6 add_convert_fusion.6
  723.4 3.8 bitcast_convert_fusion
  727.3 8.0 convert_reduce_fusion.6
  736.3 2.6 convolution_convert_fusion
  743.4 4.5 fusion.128
  755.0 2.7 fusion.317
  757.7 3.0 fusion.114
  760.7 3.3 fusion.120
  765.9 9.8 fusion.241
  775.6 5.9 copy.100
  781.6 2.9 copy.110
  786.9 98.8 %all-reduce.20.cloned.1.call-done = (bf16[1024,1024]{1,0:T(8,128)(2,1)}, bf16[1024,1024]{1,0:T(8,128)(2,1)}, bf16[1024,1024]{1,0:T(8,128)(2,1)}) async-done(((bf16[1024,1024]{1,0:T(8,128)(2,1)}, bf16[1024,1024]{1,0:T(8,128)(2,1)}, bf16[1024,1024]{1,0:T(8,128)(2,1)}), (bf16[1024,1024]{1,0:T(8,128)(2,1)}, bf16[1024,1024]{1,0:T(8,128)(2,1)}, bf16[1024,1024]{1,0:T(8,128)(2,1)})) %all-reduce.20.cloned.1.call-update) | async-done | bytes 6291472 | tf_op jit(solution)/shard_map/psum | solution.py:218
  885.7 6.5 fusion.71
  897.2 26.0 %reduce-scatter.15.cloned.1.call-done = bf16[128,128]{1,0:T(8,128)(2,1)} async-done(((bf16[1024,128]{1,0:T(8,128)(2,1)}), bf16[128,128]{1,0:T(8,128)(2,1)}) %reduce-scatter.15.cloned.1.call-update) | async-done | bytes 32784
  924.7 39.1 %reduce-scatter.17.cloned.1.call-done = bf16[128,512]{1,0:T(8,128)(2,1)} async-done(((bf16[1024,512]{1,0:T(8,128)(2,1)}), bf16[128,512]{1,0:T(8,128)(2,1)}) %reduce-scatter.17.cloned.1.call-update) | async-done | bytes 131088
  965.9 6.2 fusion.249
  972.3 32.8 %all-reduce.6 = (f32[1,2,1024]{2,1,0:T(2,128)}, f32[1,2,1024]{2,1,0:T(2,128)}, f32[1,3,128]{2,0,1:T(1,128)}, f32[1,512]{1,0:T(1,128)}, f32[1,1024]{1,0:T(1,128)}) all-reduce(f32[1,2,1024]{2,1,0:T(2,128)S(1)} %fusion.550, f32[1,2,1024]{2,1,0:T(2,128)S(1)} %fusion.551, ...), channel_id=1, replica_groups=mesh['section'=2,'dp'=8,'tensor'=8] {'dp'}, use_global_device_ids=true, to_apply=%region_57.58 | all-reduce | flops 6016 | bytes 48128 | tf_op jit(solution)/shard_map/psum | solution.py:338
  1005.1 2.8 add_bitcast_fusion
  1008.6 4.2 fusion.47
  1012.8 3.7 fusion
  1018.3 26.3 %reduce-scatter.11.cloned.1.call-done = bf16[1,128,512]{2,1,0:T(8,128)(2,1)} async-done(((bf16[1,1024,512]{2,1,0:T(8,128)(2,1)}), bf16[1,128,512]{2,1,0:T(8,128)(2,1)}) %reduce-scatter.11.cloned.1.call-update) | async-done | bytes 131088 | tf_op jit(solution)/shard_map/reduce_scatter | solution.py:331
  (678 shorter events, 169.4 us)
Async XLA Ops:
  7.2 84.2 %all-gather.3.cloned.1.call-start = ((), (), s32[]{:S(2)}) async-start(), calls=%async_computation.4 | async-start | bytes 1179648 | tf_op jit(solution)/shard_map/all_gather | solution.py:240
  7.9 101.3 %all-gather.5.cloned.1.call-start = ((), (), s32[]{:S(2)}) async-start(), calls=%async_computation.5 | async-start | bytes 1179648 | tf_op jit(solution)/shard_map/all_gather | solution.py:241
  8.7 201.9 %all-reduce.16.cloned.1.call-start = ((), (), s32[]{:S(2)}) async-start(), calls=%async_computation.6 | async-start | bytes 4194304 | tf_op jit(solution)/shard_map/psum | solution.py:170
  9.5 45.4 %copy-start.147 = (f32[1,3,128]{2,1,0:T(4,128)}, f32[1,3,128]{2,1,0:T(4,128)S(1)}, u32[]{:S(2)}) copy-start(f32[1,3,128]{2,1,0:T(4,128)S(1)} %copy.113) | copy-start | bytes 4612
  11.7 209.9 %copy-start.130 = (f32[1,1,1024]{2,1,0:T(1,128)}, f32[1,1,1024]{2,1,0:T(1,128)S(1)}, u32[]{:S(2)}) copy-start(f32[1,1,1024]{2,1,0:T(1,128)S(1)} %get-tuple-element.352) | copy-start | bytes 12292
  17.1 37.8 %copy-start.187 = (f32[1024]{0:T(1024)}, f32[1024]{0:T(1024)S(1)}, u32[]{:S(2)}) copy-start(f32[1024]{0:T(1024)S(1)} %add_rsqrt_fusion.5) | copy-start | bytes 12292
  55.1 31.9 %copy-start.82 = (bf16[1,1024,128]{1,2,0:T(8,128)(2,1)}, bf16[1,1024,128]{1,2,0:T(8,128)(2,1)S(1)}, u32[]{:S(2)}) copy-start(bf16[1,1024,128]{1,2,0:T(8,128)(2,1)S(1)} %slice.1188) | copy-start | bytes 786436
  58.0 30.5 %copy-start.109 = (bf16[2,64,512]{2,1,0:T(8,128)(2,1)}, bf16[2,64,512]{2,1,0:T(8,128)(2,1)S(1)}, u32[]{:S(2)}) copy-start(bf16[2,64,512]{2,1,0:T(8,128)(2,1)S(1)} %convolution_convert_fusion.6) | copy-start | bytes 393220
  59.2 27.9 %copy-start.156 = (f32[2,512]{1,0:T(2,128)}, f32[2,512]{1,0:T(2,128)S(1)}, u32[]{:S(2)}) copy-start(f32[2,512]{1,0:T(2,128)S(1)} %get-tuple-element.355) | copy-start | bytes 12292
  60.3 28.2 %copy-start.157 = (f32[2,512]{1,0:T(2,128)}, f32[2,512]{1,0:T(2,128)S(1)}, u32[]{:S(2)}) copy-start(f32[2,512]{1,0:T(2,128)S(1)} %fusion.84) | copy-start | bytes 12292
  91.3 17.9 %copy-start.203 = (f32[1,512]{1,0:T(1,128)S(1)}, f32[1,512]{1,0:T(1,128)}, u32[]{:S(2)}) copy-start(f32[1,512]{1,0:T(1,128)} %param.53) | copy-start | bytes 6148
  94.5 23.1 %copy-start.219 = (f32[1024,512]{1,0:T(8,128)}, f32[1024,512]{1,0:T(8,128)S(1)}, u32[]{:S(2)}) copy-start(f32[1024,512]{1,0:T(8,128)S(1)} %fusion.123) | copy-start | bytes 6291460
  117.7 92.9 %copy-start.128 = (f32[1,1024]{1,0:T(1,128)S(1)}, f32[1,1024]{1,0:T(1,128)}, u32[]{:S(2)}) copy-start(f32[1,1024]{1,0:T(1,128)} %param.55) | copy-start | bytes 12292
  117.7 214.9 %all-reduce.18.cloned.1.call-start = ((), (), s32[]{:S(2)}) async-start(), calls=%async_computation.7 | async-start | bytes 4194304 | tf_op jit(solution)/shard_map/psum | solution.py:170
  210.6 8.5 copy-start
  214.0 5.1 collective-permute-start
  241.0 271.4 %all-reduce.24.cloned.1.call-start = ((), (), s32[]{:S(2)}) async-start(), calls=%async_computation.14 | async-start | bytes 8388608 | tf_op jit(solution)/shard_map/psum | solution.py:218
  336.5 5.1 collective-permute-start.2
  354.8 9.8 copy-start.47
  383.7 13.3 %copy-start.2 = (bf16[1,2048,1024]{2,1,0:T(8,128)(2,1)S(1)}, bf16[1,2048,1024]{2,1,0:T(8,128)(2,1)}, u32[]{:S(2)}) copy-start(bf16[1,2048,1024]{2,1,0:T(8,128)(2,1)} %param.46) | copy-start | bytes 12582916
  383.7 13.3 %copy-start.200 = (bf16[1,512,1024]{2,1,0:T(8,128)(2,1)S(1)}, bf16[1,512,1024]{2,1,0:T(8,128)(2,1)}, u32[]{:S(2)}) copy-start(bf16[1,512,1024]{2,1,0:T(8,128)(2,1)} %all-gather.5.cloned.1.call-done) | copy-start | bytes 3145732
  403.2 274.1 %all-reduce.22.cloned.1.call-start = ((), (), s32[]{:S(2)}) async-start(), calls=%async_computation.13 | async-start | bytes 8388608 | tf_op jit(solution)/shard_map/psum | solution.py:217
  512.4 7.7 copy-start.3
  512.4 7.7 copy-start.32
  512.4 7.7 copy-start.33
  512.4 7.7 copy-start.136
  522.8 7.7 collective-permute-start.1
  525.2 11.1 %copy-start.49 = (bf16[1,1024,128]{1,2,0:T(8,128)(2,1)}, bf16[1,1024,128]{1,2,0:T(8,128)(2,1)S(1)}, u32[]{:S(2)}) copy-start(bf16[1,1024,128]{1,2,0:T(8,128)(2,1)S(1)} %slice.1186) | copy-start | bytes 786436
  567.6 318.0 %all-reduce.20.cloned.1.call-start = ((), (), s32[]{:S(2)}) async-start(), calls=%async_computation.12 | async-start | bytes 12582912 | tf_op jit(solution)/shard_map/psum | solution.py:218
  677.3 10.0 copy-start.4
  677.3 10.0 copy-start.8
  677.3 10.0 copy-start.20
  677.3 10.0 copy-start.25
  677.3 10.0 copy-start.26
  677.3 10.0 copy-start.27
  677.3 10.0 copy-start.134
  687.4 7.1 copy-start.117
  687.4 7.1 copy-start.119
  692.7 10.3 collective-permute-start.3
  727.3 9.0 copy-start.198
  739.0 184.2 %reduce-scatter.15.cloned.1.call-start = ((), (), s32[]{:S(2)}) async-start(), calls=%async_computation.10 | async-start | bytes 294912
  765.6 198.2 %reduce-scatter.17.cloned.1.call-start = ((), (), s32[]{:S(2)}) async-start(), calls=%async_computation.11 | async-start | bytes 1179648
  784.5 101.2 %copy-start.133 = (f32[1024]{0:T(1024)S(1)}, f32[1024]{0:T(1024)}, u32[]{:S(2)}) copy-start(f32[1024]{0:T(1024)} %broadcast_multiply_fusion.7) | copy-start | bytes 12292
  784.5 231.9 %reduce-scatter.13.cloned.1.call-start = ((), (), s32[]{:S(2)}) async-start(), calls=%async_computation.9 | async-start | bytes 884736
  885.7 8.6 copy-start.21
  885.7 8.6 copy-start.93
  897.1 147.5 %reduce-scatter.11.cloned.1.call-start = ((), (), s32[]{:S(2)}) async-start(), calls=%async_computation.8 | async-start | bytes 1179648 | tf_op jit(solution)/shard_map/reduce_scatter | solution.py:331
  965.9 39.2 %copy-start.10 = (bf16[1024,1024]{1,0:T(8,128)(2,1)S(1)}, bf16[1024,1024]{1,0:T(8,128)(2,1)}, u32[]{:S(2)}) copy-start(bf16[1024,1024]{1,0:T(8,128)(2,1)} %copy-done.6) | copy-start | bytes 6291460
  (188 other events, 521.2 us)
Sparse Core Ops, SparseCore 0:
  9.7 50.9 all-gather.2
  62.2 46.9 all-gather.4
  117.8 92.7 all-reduce.15
  241.1 91.4 all-reduce.17
  403.3 109.0 all-reduce.23
  567.8 109.4 all-reduce.21
  739.1 146.5 all-reduce.19
  888.6 34.5 reduce-scatter.14
  925.7 38.1 reduce-scatter.16
  966.2 37.3 reduce-scatter.12
  1006.0 38.6 reduce-scatter.10
where the time goes:
time: 1060 us; the launch traced here: 1050 us
  waiting for transfers between devices  601 us (57%)
  matrix products  168 us (16%)
  other arithmetic  110 us (10%)
  blocking collectives  94 us (9%)
  local copies, waits for them, and re-layouts  55.6 us (5%)
  between operations  17.2 us (2%)
    psum x2, waiting for transfers between devices, layer_backward(): lax.psum(d_second.astype(jnp.bfloat16), 'tensor').astype(jnp.float32)  207 us
    psum x2, waiting for transfers between devices, layer_forward(): lax.psum(partial_sum.astype(jnp.bfloat16), 'tensor').astype(jnp.float32)  184 us
    psum x1, waiting for transfers between devices, layer_backward(): lax.psum(d_first.astype(jnp.bfloat16), 'tensor').astype(jnp.float32)  98.4 us
    unnamed x14, waiting for transfers between devices  66.6 us
    unnamed x457, local copies, waits for them, and re-layouts  36.3 us
    all_gather x1, blocking collectives, fetch_each(): lax.all_gather(shards[0], 'dp', axis=2, tiled=True)  34.5 us
    psum x1, blocking collectives, body(): lax.psum((small_sums[0][None], small_sums[1][None], small_sums[2][None],...  32.8 us
    all_gather x1, blocking collectives, fetch_each(): lax.all_gather(shards[1], 'dp', axis=2, tiled=True)  26.7 us
  transfers between devices with their start and end apart: 15, of which 11 were waited for; matrix products, arithmetic and copies ran while one was open for 12% of the time, Pallas kernels for 0%

commit v1 on v0

v1 whole, which is shorter than its diff:
```python
import functools

import jax
import jax.numpy as jnp
import numpy as np
from jax import lax
from jax.experimental import pallas as pl
from jax.experimental.pallas import tpu as pltpu
from jax.sharding import PartitionSpec as P

MESH = pl.DeviceIdType.MESH
BF = jnp.bfloat16
F32 = jnp.float32

D = 1024
LEN = 1024
HD = 64
ROT = 16
NIN = 896
NOUT = 640
NALL = NIN + NOUT
BQ = 256
NCH = 2
R = LEN // NCH
HALF = R // 2
QUARTER = R // 8
BM = min(256, HALF)
NB = HALF // BM
W_PARTS = (((0, NIN), (NIN, NALL)), ((0, NALL),))
G_PARTS = ((384, NALL), (0, 384))


def dot(a, b, ca, cb):
    return lax.dot_general(a, b, (((ca,), (cb,)), ((), ())), preferred_element_type=F32)


def rotary_tables():
    position = np.arange(LEN, dtype=np.float32)[:, None]
    exponent = np.arange(ROT // 2, dtype=np.float32) * np.float32(2.0) / np.float32(ROT)
    angles = (position * np.float32(10000.0) ** (-exponent)).astype(np.float32)
    cosine = np.ones((LEN, 2 * HD), np.float32)
    sine = np.zeros((LEN, 2 * HD), np.float32)
    for first in (0, 8, HD, HD + 8):
        cosine[:, first : first + 8] = np.cos(angles)
        sine[:, first : first + 8] = np.sin(angles)
    return cosine, sine


def lanes_of_head(shape):
    return lax.broadcasted_iota(jnp.int32, shape, 1) % HD


def turn(value, cosine, sine):
    lane = lanes_of_head(value.shape)
    partner = jnp.where(lane < 8, -pltpu.roll(value, 120, 1), pltpu.roll(value, 8, 1))
    return value * cosine + partner * sine


def turn_back(grad, cosine, sine):
    lane = lanes_of_head(grad.shape)
    moved = grad * sine
    partner = jnp.where(
        lane < 8, pltpu.roll(moved, 120, 1), jnp.where(lane < 16, -pltpu.roll(moved, 8, 1), 0.0)
    )
    return grad * cosine + partner


def gelu_and_slope(hidden):
    bell = jnp.exp(-0.5 * hidden * hidden)
    size = 1.0 + (0.3275911 * 0.7071067811865476) * jnp.abs(hidden)
    t = pltpu.reciprocal(size, approx=True)
    t = t * (2.0 - size * t)
    series = t * (
        0.254829592 * 0.5
        + t
        * (
            -0.284496736 * 0.5
            + t * (1.421413741 * 0.5 + t * (-1.453152027 * 0.5 + t * (1.061405429 * 0.5)))
        )
    )
    tail = series * bell
    below = jnp.where(hidden >= 0.0, 1.0 - tail, tail)
    return hidden * below, below + hidden * bell * 0.3989422804014327


def standardize(value):
    center = jnp.mean(value, axis=-1, keepdims=True)
    centred = value - center
    inverse = lax.rsqrt(jnp.mean(centred * centred, axis=-1, keepdims=True) + 1e-05)
    return centred * inverse, inverse


def stack_heads(value):
    lane = lax.broadcasted_iota(jnp.int32, value.shape, 1)
    wide = value.astype(F32)
    return jnp.concatenate(
        [jnp.where(lane < HD, wide, 0.0), jnp.where(lane >= HD, wide, 0.0)], axis=0
    ).astype(BF)


def split_heads(value):
    half = value.shape[1] // 2
    return jnp.concatenate([value[:HD, :half], value[HD:, half:]], axis=0)


def pair(i, j):
    return i * (i + 1) // 2 + j


def kernel(
    ends,
    qkv,
    dense,
    up,
    down,
    gains,
    offsets,
    qkv_b,
    up_b,
    out_b,
    cosine,
    sine,
    ends_out,
    g_gains,
    g_offsets,
    g_qkv,
    g_qkv_b,
    g_dense,
    g_up,
    g_up_b,
    g_down,
    g_out_b,
    shard,
    extra,
    extras,
    bias_row,
    out_row,
    weights,
    x_in,
    grads_in,
    xhat,
    y_mid,
    joined,
    slope,
    queries,
    keys,
    values,
    keys_t,
    values_t,
    soft,
    soft_scale,
    context_t,
    scores,
    d_context,
    d_joined,
    d_keys,
    d_values,
    part,
    core_part,
    ring_part,
    ends_low,
    w_grad,
    plane_a,
    plane_b,
    sum_a,
    sum_b,
    own_a,
    own_b,
    total,
    message,
    messages,
    bias_total,
    ln_own,
    ln_ring,
    ln_plane,
    local_sem,
    swap_s,
    swap_r,
    w1_s,
    w_r,
    w2a_s,
    w2b_s,
    extra_s,
    extra_r,
    core_s,
    core_r,
    ring_s,
    ring_r,
    gx_s,
    gx_r,
    gc_s,
    gc_r,
    out_s,
    out_r,
    across_s,
    across_r,
    direct_s,
    direct_r,
    direct2_s,
    direct2_r,
    msg_s,
    msg_r,
    p1a_s,
    p1a_r,
    p1b_s,
    p1b_r,
    p2a_s,
    p2a_r,
    p2b_s,
    p2b_r,
    ln1_s,
    ln1_r,
    ln2_s,
    ln2_r,
):
    core = lax.axis_index("section")
    dp = lax.axis_index("dp")
    t = lax.axis_index("tensor")
    y, z_lo = dp // 2, dp % 2
    z_hi, x = t // 4, t % 4
    z = 2 * z_hi + z_lo
    forwarder = core == z_hi

    def device(c_, y_, z_, x_):
        return {"section": c_, "dp": y_ * 2 + z_ % 2, "tensor": (z_ // 2) * 4 + x_}

    drains = {}

    def wait(ref, sem):
        pltpu.make_async_copy(ref, ref, sem).wait()

    def push(src, dst, send, recv, where, tag="end"):
        pltpu.make_async_remote_copy(
            src_ref=src, dst_ref=dst, send_sem=send, recv_sem=recv, device_id=where, device_id_type=MESH
        ).start()
        drains.setdefault(tag, []).append((None, src, send))

    def push_or_keep(own, src, dst, send, recv, where):
        other = jnp.logical_not(own)

        @pl.when(own)
        def _():
            pltpu.make_async_copy(src, dst, recv).start()

        @pl.when(other)
        def _():
            pltpu.make_async_remote_copy(
                src_ref=src,
                dst_ref=dst,
                send_sem=send,
                recv_sem=recv,
                device_id=where,
                device_id_type=MESH,
            ).start()

        drains.setdefault("end", []).append((other, src, send))

    def drain(tag):
        for condition, src, send in drains.pop(tag, []):
            if condition is None:
                wait(src, send)
            else:
                pl.when(condition)(functools.partial(wait, src, send))

    barrier = pltpu.get_barrier_semaphore()
    for dy in range(4):
        for dz in range(4):
            for c_ in range(2):
                if (dy, dz, c_) == (0, 0, 0):
                    continue
                pl.semaphore_signal(
                    barrier,
                    inc=1,
                    device_id=device((core + c_) % 2, (y + dy) % 4, (z + dz) % 4, x),
                    device_id_type=MESH,
                )
    for j in range(1, 4):
        pl.semaphore_signal(
            barrier, inc=1, device_id=device(core, y, z, (x + j) % 4), device_id_type=MESH
        )

    block = pl.ds(pl.multiple_of(dp * 128, 128), 128)

    def column(row):
        return jnp.broadcast_to(row, (128, 128)).T

    gain_cols = [column(gains[k : k + 1, block]) for k in range(2)]
    offset_cols = [column(offsets[k : k + 1, block]) for k in range(2)]

    def raw_tile(n):
        if n < 3:
            return qkv[n].astype(F32), 0, qkv_b[n]
        cols = slice((n - 3) * 128, (n - 2) * 128)
        return up[:, cols].astype(F32), 1, up_b[:, cols]

    extra[...] = jnp.zeros_like(extra)
    for n in range(7):
        tile, k, bias = raw_tile(n)
        shard[:, n * 128 : (n + 1) * 128] = (tile * gain_cols[k]).astype(BF)
        added = jnp.sum(tile * offset_cols[k], axis=0, keepdims=True) + 0.125 * bias
        extra[n // 2 : n // 2 + 1, (n % 2) * 128 : (n % 2) * 128 + 128] = added
    for n in range(4):
        extra[4 + n : 5 + n, :] = 0.125 * out_b[:, n * 256 : (n + 1) * 256]
    shard[:, NIN : NIN + 128] = dense[...].T
    shard[:, NIN + 128 : NALL] = down[...].T

    pl.semaphore_wait(barrier, 34)

    mine = ends.at[pl.ds(pl.multiple_of(z_hi * LEN, LEN), LEN)]
    for c_, buffer in ((0, x_in), (1, grads_in.at[1])):

        @pl.when(core == c_)
        def _(buffer=buffer):
            pltpu.make_async_copy(mine, buffer, local_sem).start()
            pltpu.make_async_remote_copy(
                src_ref=mine,
                dst_ref=buffer,
                send_sem=swap_s,
                recv_sem=swap_r,
                device_id=device(1 - core, y, z, x),
                device_id_type=MESH,
            ).start()

    def w_rows(l, p, dp_, half):
        rows = pl.ds(pl.multiple_of(dp_ * 128 + half * 64, 64), 64)
        return weights.at[l, rows, slice(*W_PARTS[l][p])]

    def gather_first(l):
        @pl.when(core == l)
        def _():
            for p, cols in enumerate(W_PARTS[l]):
                for half in range(2):
                    src = shard.at[half * 64 : half * 64 + 64, slice(*cols)]
                    dst = w_rows(l, p, dp, half)
                    recv = w_r.at[half, l, p, dp]

                    @pl.when(forwarder)
                    def _(src=src, dst=dst, recv=recv):
                        pltpu.make_async_copy(src, dst, recv).start()

                    for j in range(4):
                        if half == 0:
                            where = device(z_hi, (y + j) % 4, z, x)
                        else:
                            where = device(z_hi, y, (z + j) % 4, x)
                        copy = pltpu.make_async_remote_copy(
                            src_ref=src,
                            dst_ref=dst,
                            send_sem=w1_s.at[p, half, j],
                            recv_sem=recv,
                            device_id=where,
                            device_id_type=MESH,
                        )
                        if j == 0:
                            pl.when(jnp.logical_not(forwarder))(copy.start)
                        else:
                            copy.start()

    def drain_first():
        for l in range(2):

            @pl.when(core == l)
            def _(l=l):
                for p, cols in enumerate(W_PARTS[l]):
                    src = shard.at[0:64, slice(*cols)]
                    for half in range(2):
                        for j in range(4):
                            ended = functools.partial(wait, src, w1_s.at[p, half, j])
                            if j == 0:
                                pl.when(jnp.logical_not(forwarder))(ended)
                            else:
                                ended()

    def gather_second(l, p):
        for k in range(2):
            block_b = w_rows(l, p, y * 2 + k, 1)
            wait(block_b, w_r.at[1, l, p, y * 2 + k])
            for j in range(1, 4):
                push(
                    block_b,
                    block_b,
                    w2b_s.at[l, p, k, j - 1],
                    w_r.at[1, l, p, y * 2 + k],
                    device(core, (y + j) % 4, z, x),
                )

        @pl.when(forwarder)
        def _():
            for y_ in range(4):
                dp_ = y_ * 2 + z_lo
                block_a = w_rows(l, p, dp_, 0)
                wait(block_a, w_r.at[0, l, p, dp_])
                for j in range(1, 4):
                    pltpu.make_async_remote_copy(
                        src_ref=block_a,
                        dst_ref=block_a,
                        send_sem=w2a_s.at[l, p, y_, j - 1],
                        recv_sem=w_r.at[0, l, p, dp_],
                        device_id=device(core, y, (z + j) % 4, x),
                        device_id_type=MESH,
                    ).start()

    def drain_second():
        @pl.when(forwarder)
        def _():
            for l in range(2):
                for p in range(len(W_PARTS[l])):
                    for y_ in range(4):
                        for j in range(3):
                            wait(w_rows(l, p, 0, 0), w2a_s.at[l, p, y_, j])

    def gather_rest(l, p):
        for j in range(1, 4):
            for k in range(2):
                dp_ = ((y + j) % 4) * 2 + k
                wait(w_rows(l, p, dp_, 1), w_r.at[1, l, p, dp_])
        for y_ in range(4):
            dp_ = y_ * 2 + 1 - z_lo
            wait(w_rows(l, p, dp_, 0), w_r.at[0, l, p, dp_])

            @pl.when(jnp.logical_not(forwarder))
            def _(dp_=y_ * 2 + z_lo):
                wait(w_rows(l, p, dp_, 0), w_r.at[0, l, p, dp_])

        if p > 0:
            return
        for dp_ in range(8):
            wait(extras.at[l, dp_], extra_r.at[l, dp_])
        summed = extras[l, 0]
        for dp_ in range(1, 8):
            summed = summed + extras[l, dp_]
        for n in range(4):
            bias_row[l, :, n * 256 : (n + 1) * 256] = summed[n : n + 1, :]
            out_row[l, :, n * 256 : (n + 1) * 256] = summed[4 + n : 5 + n, :]

    gather_first(0)
    for l in range(2):

        @pl.when(core == l)
        def _(l=l):
            for dy in range(4):
                for dz in range(4):
                    where = device(z_hi, (y + dy) % 4, (z + dz) % 4, x)
                    dst = extras.at[l, dp]
                    recv = extra_r.at[l, dp]
                    copy = pltpu.make_async_remote_copy(
                        src_ref=extra,
                        dst_ref=dst,
                        send_sem=extra_s.at[dy * 4 + dz],
                        recv_sem=recv,
                        device_id=where,
                        device_id_type=MESH,
                    )
                    if (dy, dz) == (0, 0):
                        pl.when(forwarder)(pltpu.make_async_copy(extra, dst, recv).start)
                        pl.when(jnp.logical_not(forwarder))(copy.start)
                    else:
                        copy.start()

    def drain_extra():
        for k in range(16):
            if k == 0:
                pl.when(jnp.logical_not(forwarder))(
                    functools.partial(wait, extra, extra_s.at[k])
                )
            else:
                wait(extra, extra_s.at[k])

    wait(x_in, local_sem)
    wait(x_in, swap_r)

    gather_second(0, 0)

    def normalize_rows(i, carry):
        rows = pl.ds(pl.multiple_of(i * 128, 128), 128)
        xhat[0, rows, :] = standardize(x_in[rows, :].astype(F32))[0].astype(BF)
        return carry

    lax.fori_loop(0, LEN // 128, normalize_rows, 0)
    gather_second(0, 1)
    gather_first(1)
    gather_rest(0, 0)

    def project(l, i):
        rows = pl.ds(pl.multiple_of(i * BQ, BQ), BQ)
        low = xhat[l, rows, :]
        raw = dot(low, weights[l, :, 0:384], 1, 0) + bias_row[l, :, 0:384]
        cos_rows, sin_rows = cosine[rows, :], sine[rows, :]
        q = turn(raw[:, 0:128], cos_rows, sin_rows) * HD**-0.5
        k = turn(raw[:, 128:256], cos_rows, sin_rows)
        v = raw[:, 256:384]
        queries[l, rows, :] = q.astype(BF)
        keys[l, rows, :] = k.astype(BF)
        values[l, rows, :] = v.astype(BF)
        keys_t[l, :, rows] = k.T.astype(BF)
        values_t[l, :, rows] = v.T.astype(BF)
        hidden = dot(low, weights[l, :, 384:NIN], 1, 0) + bias_row[l, :, 384:NIN]
        act, gradient = gelu_and_slope(hidden)
        joined[l, rows, 128:NOUT] = act.astype(BF)
        slope[l, rows, :] = gradient.astype(BF)

    def attend(l, i):
        rows = slice(i * BQ, (i + 1) * BQ)
        stacked = stack_heads(queries[l, rows, :])
        largest = None
        for j in range(i + 1):
            tile = dot(keys[l, j * BQ : (j + 1) * BQ, :], stacked, 1, 1)
            if j == i:
                key_at = lax.broadcasted_iota(jnp.int32, tile.shape, 0)
                query_at = lax.broadcasted_iota(jnp.int32, tile.shape, 1) % BQ
                tile = jnp.where(key_at <= query_at, tile, -1e30)
            scores[j * BQ : (j + 1) * BQ, :] = tile
            top = jnp.max(tile, axis=0, keepdims=True)
            largest = top if largest is None else jnp.maximum(largest, top)
        summed = jnp.zeros((1, 2 * BQ), F32)
        outcome = jnp.zeros((2 * HD, 2 * BQ), F32)
        for j in range(i + 1):
            terms = jnp.exp(scores[j * BQ : (j + 1) * BQ, :] - largest)
            summed = summed + jnp.sum(terms, axis=0, keepdims=True)
            low = terms.astype(BF)
            soft[l, pair(i, j)] = low
            outcome = outcome + dot(values_t[l, :, j * BQ : (j + 1) * BQ], low, 1, 0)
        scale = 1.0 / summed
        soft_scale[l, i : i + 1, :] = scale
        context = split_heads(outcome * scale)
        context_t[l, :, rows] = context
        joined[l, rows, 0:128] = context.T.astype(BF)

    def attend_back(l, i):
        rows = slice(i * BQ, (i + 1) * BQ)
        grad_t = d_context[rows, :].astype(F32).T
        scale = soft_scale[l, i : i + 1, :]
        top = grad_t[:HD] * scale[:, :BQ]
        bottom = grad_t[HD:] * scale[:, BQ:]
        context = context_t[l, :, rows]
        delta = jnp.concatenate(
            [
                jnp.sum(context[:HD] * top, axis=0, keepdims=True),
                jnp.sum(context[HD:] * bottom, axis=0, keepdims=True),
            ],
            axis=1,
        )
        blank = jnp.zeros_like(top)
        spread_wide = jnp.concatenate(
            [jnp.concatenate([top, blank], axis=1), jnp.concatenate([blank, bottom], axis=1)], axis=0
        )
        spread_t = spread_wide.astype(BF)
        spread = spread_wide.T.astype(BF)
        stacked = stack_heads(queries[l, rows, :])
        d_query_t = jnp.zeros((2 * HD, 2 * BQ), F32)
        for j in range(i + 1):
            cols = slice(j * BQ, (j + 1) * BQ)
            terms = soft[l, pair(i, j)]
            d_terms = dot(values[l, cols, :], spread_t, 1, 0)
            d_scores = (terms.astype(F32) * (d_terms - delta)).astype(BF)
            d_key = dot(d_scores, stacked, 1, 0)
            d_value = dot(terms, spread, 1, 0)
            if i == LEN // BQ - 1:
                d_keys[cols, :] = d_key
                d_values[cols, :] = d_value
            else:
                d_keys[cols, :] += d_key
                d_values[cols, :] += d_value
            d_query_t = d_query_t + dot(keys_t[l, :, cols], d_scores, 1, 0)
        d_query = split_heads(d_query_t).T * HD**-0.5
        d_joined[rows, 0:128] = turn_back(d_query, cosine[rows, :], sine[rows, :]).astype(BF)

    def finish_keys(i, carry):
        rows = pl.ds(pl.multiple_of(i * BQ, BQ), BQ)
        d_joined[rows, 128:256] = turn_back(d_keys[rows, :], cosine[rows, :], sine[rows, :]).astype(
            BF
        )
        d_joined[rows, 256:384] = d_values[rows, :].astype(BF)
        return carry

    def blocks_of(ck):
        return range(ck * R // BQ, (ck + 1) * R // BQ)

    def forward(l, ck):
        def one(i, carry):
            project(l, i)
            return carry

        lax.fori_loop(ck * R // BQ, (ck + 1) * R // BQ, one, 0)
        for i in blocks_of(ck):
            attend(l, i)

    def backward_first(l, ck):
        def one(i, carry):
            rows = pl.ds(pl.multiple_of(i * BQ, BQ), BQ)
            both = dot(grads_in[l, rows, :], weights[l, :, NIN:NALL], 1, 0)
            d_context[rows, :] = both[:, 0:128].astype(BF)
            d_joined[rows, 384:NIN] = (both[:, 128:NOUT] * slope[l, rows, :].astype(F32)).astype(BF)
            return carry

        lax.fori_loop(ck * R // BQ, (ck + 1) * R // BQ, one, 0)

    def backward_second(l, ck):
        for i in reversed(blocks_of(ck)):
            attend_back(l, i)
        lax.fori_loop(ck * R // BQ, (ck + 1) * R // BQ, finish_keys, 0)

    def branch(l, rows):
        return dot(joined[l, rows, :], weights[l, :, NIN:NALL], 1, 1)

    def norm_grad(l, rows):
        return dot(d_joined[rows, :], weights[l, :, 0:NIN], 1, 1)

    def own_rows(ck, part_=None):
        first = ck * R + core * HALF + x * QUARTER
        return pl.ds(pl.multiple_of(first, QUARTER), QUARTER)

    def reduce_send(ph, ck, term):
        slot = ph % 2
        drain(("part", ck))
        for b in range(NB):
            rows = pl.ds(pl.multiple_of(ck * R + (1 - core) * HALF + b * BM, BM), BM)
            part[rows, :] = term(rows).astype(BF)
            push(
                part.at[rows],
                core_part.at[slot, ck * HALF + b * BM : ck * HALF + (b + 1) * BM],
                core_s.at[ph, ck, b],
                core_r.at[ph, ck, b],
                device(1 - core, y, z, x),
                ("part", ck),
            )
        for b in range(NB):
            rows = pl.ds(pl.multiple_of(ck * R + core * HALF + b * BM, BM), BM)
            value = term(rows)
            other = core_part.at[slot, ck * HALF + b * BM : ck * HALF + (b + 1) * BM]
            wait(other, core_r.at[ph, ck, b])
            part[rows, :] = (value + other[...].astype(F32)).astype(BF)
        for j in range(1, 4):
            to = (x + j) % 4
            first = ck * R + core * HALF + to * QUARTER
            push(
                part.at[pl.ds(pl.multiple_of(first, QUARTER), QUARTER)],
                ring_part.at[slot, j - 1, ck * QUARTER : (ck + 1) * QUARTER],
                ring_s.at[ph, ck, j - 1],
                ring_r.at[ph, ck, j - 1],
                device(core, y, z, to),
                ("part", ck),
            )

    def reduce_finish(ph, ck):
        slot = ph % 2
        summed = part[own_rows(ck), :].astype(F32)
        for j in range(3):
            piece = ring_part.at[slot, j, ck * QUARTER : (ck + 1) * QUARTER]
            wait(piece, ring_r.at[ph, ck, j])
            summed = summed + piece[...].astype(F32)
        return summed

    def gather_send(n, ck, buffer):
        rows = own_rows(ck)
        for j in range(1, 4):
            push(
                buffer.at[rows],
                buffer.at[rows],
                gx_s.at[n, ck, j - 1],
                gx_r.at[n, ck, j - 1],
                device(core, y, z, (x + j) % 4),
            )
        push(
            buffer.at[rows],
            buffer.at[rows],
            gc_s.at[n, ck, 0],
            gc_r.at[n, ck, 0],
            device(1 - core, y, z, x),
        )

    def gather_pass(n, ck, buffer):
        for j in range(1, 4):
            first = ck * R + core * HALF + ((x - j + 4) % 4) * QUARTER
            piece = buffer.at[pl.ds(pl.multiple_of(first, QUARTER), QUARTER)]
            wait(piece, gx_r.at[n, ck, j - 1])
            push(
                piece,
                piece,
                gc_s.at[n, ck, j],
                gc_r.at[n, ck, j],
                device(1 - core, y, z, x),
            )

    def gather_finish(n, ck, buffer):
        for j in range(4):
            wait(buffer.at[own_rows(ck)], gc_r.at[n, ck, j])

    def out_rows(seq, ck, c_, x_):
        first = seq * LEN + ck * R + c_ * HALF + x_ * QUARTER
        return ends_out.at[pl.ds(pl.multiple_of(first, QUARTER), QUARTER)]

    def give_out(n, ck):
        src = ends_low.at[n, ck * QUARTER : (ck + 1) * QUARTER]
        dst = out_rows(z_hi, ck, core, x)
        recv = out_r.at[ck, core * 4 + x]
        target = 1 - n
        for j in range(4):
            where, send = device(target, y, z, (x + j) % 4), out_s.at[n, ck, j]
            if j == 0:
                push_or_keep(core == target, src, dst, send, recv, where)
            else:
                push(src, dst, send, recv, where)

    def out_arrived(ck):
        for c_ in range(2):
            for x_ in range(4):
                wait(out_rows(z_hi, ck, c_, x_), out_r.at[ck, c_ * 4 + x_])

    def across_copy(n, ck):
        first = z_hi * LEN + ck * R
        rows = ends_out.at[pl.ds(pl.multiple_of(first, R), R)]
        return pltpu.make_async_remote_copy(
            src_ref=rows,
            dst_ref=rows,
            send_sem=across_s.at[ck],
            recv_sem=across_r.at[ck],
            device_id=device(1 - n, y, (z + 2) % 4, x),
            device_id_type=MESH,
        )

    def across(n, ck):
        @pl.when(core == 1 - n)
        def _():
            out_arrived(ck)
            across_copy(n, ck).start()

    def across_end(n, ck):
        @pl.when(core == 1 - n)
        def _():
            across_copy(n, ck).wait()

    def direct_first(n, ck):
        push(
            ends_low.at[n, ck * QUARTER : (ck + 1) * QUARTER],
            out_rows(z_hi, ck, core, x),
            direct_s.at[0],
            direct_r.at[core],
            device(1 - n, y, (z + 2) % 4, x),
        )

    def direct_copy(n, ck, c_, j):
        rows = out_rows(1 - z_hi, ck, c_, x)
        return pltpu.make_async_remote_copy(
            src_ref=rows,
            dst_ref=rows,
            send_sem=direct2_s.at[c_, j - 1],
            recv_sem=direct2_r.at[c_, j - 1],
            device_id=device(1 - n, y, z, (x + j) % 4),
            device_id_type=MESH,
        )

    def direct_second(n, ck):
        @pl.when(core == 1 - n)
        def _():
            for c_ in range(2):
                wait(out_rows(1 - z_hi, ck, c_, x), direct_r.at[c_])
                for j in range(1, 4):
                    direct_copy(n, ck, c_, j).start()

    def direct_end(n, ck):
        @pl.when(core == 1 - n)
        def _():
            out_arrived(ck)
            for c_ in range(2):
                for j in range(1, 4):
                    direct_copy(n, ck, c_, j).wait()

    def weight_grads(l, p):
        for i in range(4):
            cols = slice(i * BQ, (i + 1) * BQ)
            if p == 0:
                pieces = [
                    ((384, NIN), dot(xhat[l, :, cols], d_joined[:, 384:NIN], 0, 0)),
                    ((NIN, NALL), dot(grads_in[l, :, cols], joined[l], 0, 0)),
                ]
            else:
                pieces = [((0, 384), dot(xhat[l, :, cols], d_joined[:, 0:384], 0, 0))]
            for (first, last), piece in pieces:
                low = piece.astype(BF)
                for k in range(2):
                    for half in range(2):
                        rows = slice((k * 2 + half) * 64, (k * 2 + half) * 64 + 64)
                        w_grad[i, k, half, :, first:last] = low[rows]

    def plane_first(l, p):
        cols = slice(*G_PARTS[p])
        for k in range(2):
            z_ = 2 * core + k
            slot = (z_ - z + 3) % 4
            src, send = w_grad.at[:, k, 0, :, cols], p1a_s.at[l, p, k]
            other = z_ != z

            @pl.when(other)
            def _(src=src, send=send, z_=z_, slot=slot):
                pltpu.make_async_remote_copy(
                    src_ref=src,
                    dst_ref=plane_a.at[l, slot, :, :, cols],
                    send_sem=send,
                    recv_sem=p1a_r.at[l, p, slot],
                    device_id=device(core, y, z_, x),
                    device_id_type=MESH,
                ).start()

            drains.setdefault("grad", []).append((other, src, send))
        for j in range(1, 4):
            to = (y + j) % 4
            push(
                w_grad.at[to, :, 1, :, cols],
                plane_b.at[l, j - 1, :, :, cols],
                p1b_s.at[l, p, j - 1],
                p1b_r.at[l, p, j - 1],
                device(core, to, z, x),
                "grad",
            )

    def plane_second(l, p):
        cols = slice(*G_PARTS[p])

        @pl.when(forwarder)
        def _():
            for j in range(3):
                wait(plane_a.at[l, j, :, :, cols], p1a_r.at[l, p, j])

            def one(y_, carry):
                summed = w_grad[y_, z_lo, 0, :, cols].astype(F32)
                for j in range(3):
                    summed = summed + plane_a[l, j, y_, :, cols].astype(F32)
                sum_a[l, y_, :, cols] = summed.astype(BF)
                return carry

            lax.fori_loop(0, 4, one, 0)
            for j in range(4):
                to = (y + j) % 4
                src, dst = sum_a.at[l, to, :, cols], own_a.at[y, :, cols]
                copy = pltpu.make_async_remote_copy(
                    src_ref=src,
                    dst_ref=dst,
                    send_sem=p2a_s.at[l, p, j],
                    recv_sem=p2a_r.at[p, y],
                    device_id=device(l, to, z, x),
                    device_id_type=MESH,
                )
                if j == 0:
                    pl.when(core == l)(pltpu.make_async_copy(src, dst, p2a_r.at[p, y]).start)
                    pl.when(core != l)(copy.start)
                else:
                    copy.start()

        for j in range(3):
            wait(plane_b.at[l, j, :, :, cols], p1b_r.at[l, p, j])
        for k in range(2):
            summed = w_grad[y, k, 1, :, cols].astype(F32)
            for j in range(3):
                summed = summed + plane_b[l, j, k, :, cols].astype(F32)
            sum_b[l, k, :, cols] = summed.astype(BF)
            z_ = 2 * core + k
            push_or_keep(
                jnp.logical_and(core == l, z_ == z),
                sum_b.at[l, k, :, cols],
                own_b.at[z, :, cols],
                p2b_s.at[l, p, k],
                p2b_r.at[p, z],
                device(l, y, z_, x),
            )

    def drain_plane():
        @pl.when(forwarder)
        def _():
            for l in range(2):
                for p, cols in enumerate(G_PARTS):
                    src = sum_a.at[l, 0, :, slice(*cols)]
                    for j in range(4):
                        ended = functools.partial(wait, src, p2a_s.at[l, p, j])
                        if j == 0:
                            pl.when(core != l)(ended)
                        else:
                            ended()

    def send_small(l):
        message[l] = jnp.zeros((8, 256), F32)
        column_sum = jnp.zeros((1, NIN), F32)
        out_sum = jnp.zeros((1, D), F32)

        def one(i, carry):
            rows = pl.ds(pl.multiple_of(i * 128, 128), 128)
            a, b = carry
            a = a + jnp.sum(d_joined[rows, :].astype(F32), axis=0, keepdims=True)
            b = b + jnp.sum(grads_in[l, rows, :].astype(F32), axis=0, keepdims=True)
            return a, b

        column_sum, out_sum = lax.fori_loop(0, LEN // 128, one, (column_sum, out_sum))
        for n in range(7):
            message[l, n // 2 : n // 2 + 1, (n % 2) * 128 : (n % 2) * 128 + 128] = column_sum[
                :, n * 128 : (n + 1) * 128
            ]
        for n in range(4):
            message[l, 4 + n : 5 + n, :] = out_sum[:, n * 256 : (n + 1) * 256]
        here = y * 4 + z
        for y_ in range(4):
            for k in range(2):
                z_ = 2 * core + k
                own = jnp.logical_and(core == l, jnp.logical_and(y_ == y, z_ == z))
                push_or_keep(
                    own,
                    message.at[l],
                    messages.at[here],
                    msg_s.at[l, y_ * 2 + k],
                    msg_r.at[here],
                    device(l, y_, z_, x),
                )

    def after_first_layer(ck):
        rows = own_rows(ck)
        result = x_in[rows, :].astype(F32) + reduce_finish(0, ck) + out_row[0]
        low = result.astype(BF)
        y_mid[ck * QUARTER : (ck + 1) * QUARTER, :] = low
        xhat[1, rows, :] = standardize(low.astype(F32))[0].astype(BF)
        gather_send(0, ck, xhat.at[1])

    def after_second_layer(ck):
        mid = slice(ck * QUARTER, (ck + 1) * QUARTER)
        result = y_mid[mid, :].astype(F32) + reduce_finish(1, ck) + out_row[1]
        ends_low[0, mid, :] = result.astype(BF)

    def through_norm(stream, grad, e):
        scaled, inverse = standardize(stream)
        return grad + inverse * (
            e
            - jnp.mean(e, axis=-1, keepdims=True)
            - scaled * jnp.mean(e * scaled, axis=-1, keepdims=True)
        )

    def input_grad_middle(ck):
        mid = slice(ck * QUARTER, (ck + 1) * QUARTER)
        rows = own_rows(ck)
        e = reduce_finish(2, ck)
        moved = through_norm(y_mid[mid, :].astype(F32), grads_in[1, rows, :].astype(F32), e)
        grads_in[0, rows, :] = moved.astype(BF)
        gather_send(1, ck, grads_in.at[0])

    def input_grad_first(ck):
        mid = slice(ck * QUARTER, (ck + 1) * QUARTER)
        rows = own_rows(ck)
        e = reduce_finish(3, ck)
        moved = through_norm(x_in[rows, :].astype(F32), grads_in[0, rows, :].astype(F32), e)
        ends_low[1, mid, :] = moved.astype(BF)

    forward(0, 0)
    gather_rest(0, 1)
    reduce_send(0, 0, functools.partial(branch, 0))
    gather_second(1, 0)
    forward(0, 1)
    after_first_layer(0)
    reduce_send(0, 1, functools.partial(branch, 0))
    gather_pass(0, 0, xhat.at[1])
    after_first_layer(1)
    gather_finish(0, 0, xhat.at[1])
    gather_rest(1, 0)
    forward(1, 0)
    reduce_send(1, 0, functools.partial(branch, 1))
    gather_pass(0, 1, xhat.at[1])
    gather_finish(0, 1, xhat.at[1])
    forward(1, 1)
    reduce_send(1, 1, functools.partial(branch, 1))

    wait(x_in, swap_s)
    backward_first(1, 1)
    backward_second(1, 1)
    after_second_layer(0)
    after_second_layer(1)
    reduce_send(2, 1, functools.partial(norm_grad, 1))
    backward_first(1, 0)
    backward_second(1, 0)
    input_grad_middle(1)
    reduce_send(2, 0, functools.partial(norm_grad, 1))
    weight_grads(1, 0)
    plane_first(1, 0)
    gather_pass(1, 1, grads_in.at[0])
    input_grad_middle(0)
    give_out(0, 1)
    give_out(0, 0)
    weight_grads(1, 1)
    plane_first(1, 1)
    send_small(1)
    gather_finish(1, 1, grads_in.at[0])

    backward_first(0, 1)
    backward_second(0, 1)
    gather_pass(1, 0, grads_in.at[0])
    reduce_send(3, 1, functools.partial(norm_grad, 0))
    gather_finish(1, 0, grads_in.at[0])
    backward_first(0, 0)
    plane_second(1, 0)
    plane_second(1, 1)
    drain("grad")
    weight_grads(0, 0)
    plane_first(0, 0)
    across(0, 1)
    across(0, 0)
    backward_second(0, 0)
    input_grad_first(1)
    give_out(1, 1)
    reduce_send(3, 0, functools.partial(norm_grad, 0))
    weight_grads(0, 1)
    plane_first(0, 1)
    input_grad_first(0)
    direct_first(1, 0)
    give_out(1, 0)
    send_small(0)
    across(1, 1)
    plane_second(0, 0)
    direct_second(1, 0)
    plane_second(0, 1)

    for k in range(16):
        wait(messages.at[k], msg_r.at[k])
    summed = messages[0]
    for k in range(1, 16):
        summed = summed + messages[k]
    for n in range(4):
        bias_total[:, n * 256 : (n + 1) * 256] = summed[n : n + 1, :]
        g_out_b[:, n * 256 : (n + 1) * 256] = summed[4 + n : 5 + n, :]
    for k in range(4):
        for p, cols in enumerate(G_PARTS):
            wait(own_a.at[k, :, slice(*cols)], p2a_r.at[p, k])
            wait(own_b.at[k, :, slice(*cols)], p2b_r.at[p, k])
    total[0:64, :] = (
        own_a[0].astype(F32) + own_a[1].astype(F32) + own_a[2].astype(F32) + own_a[3].astype(F32)
    )
    total[64:128, :] = (
        own_b[0].astype(F32) + own_b[1].astype(F32) + own_b[2].astype(F32) + own_b[3].astype(F32)
    )
    by_gain = [jnp.zeros((128, 128), F32) for _ in range(2)]
    by_offset = [jnp.zeros((128, 128), F32) for _ in range(2)]
    for n in range(7):
        tile, k, _ = raw_tile(n)
        cols = slice(n * 128, (n + 1) * 128)
        raw = total[:, cols]
        bias = bias_total[:, cols]
        grad = raw * gain_cols[k] + offset_cols[k] * bias
        by_gain[k] = by_gain[k] + tile * raw
        by_offset[k] = by_offset[k] + tile * bias
        if n < 3:
            g_qkv[n] = grad
            g_qkv_b[n] = bias
        else:
            g_up[:, (n - 3) * 128 : (n - 2) * 128] = grad
            g_up_b[:, (n - 3) * 128 : (n - 2) * 128] = bias
    g_dense[...] = total[:, NIN : NIN + 128].T
    g_down[...] = total[:, NIN + 128 : NALL].T
    ln_own[...] = jnp.zeros_like(ln_own)
    for n, value in enumerate(by_gain + by_offset):
        ln_own[n : n + 1, :] = jnp.sum(value.T, axis=0, keepdims=True)
    for j in range(1, 4):
        push(
            ln_own,
            ln_ring.at[j - 1],
            ln1_s.at[j - 1],
            ln1_r.at[j - 1],
            device(core, y, z, (x + j) % 4),
        )
    for j in range(3):
        wait(ln_ring.at[j], ln1_r.at[j])
    here = y * 4 + z
    ln_plane[here] = ln_own[...] + ln_ring[0] + ln_ring[1] + ln_ring[2]
    for dy in range(4):
        for dz in range(4):
            if (dy, dz) != (0, 0):
                push(
                    ln_plane.at[here],
                    ln_plane.at[here],
                    ln2_s.at[dy * 4 + dz - 1],
                    ln2_r.at[here],
                    device(core, (y + dy) % 4, (z + dz) % 4, x),
                )
    for dy in range(4):
        for dz in range(4):
            if (dy, dz) != (0, 0):
                there = ((y + dy) % 4) * 4 + (z + dz) % 4
                wait(ln_plane.at[there], ln2_r.at[there])
    for dp_ in range(8):
        first = (dp_ // 2) * 4 + dp_ % 2
        both = ln_plane[first] + ln_plane[first + 2]
        cols = slice(dp_ * 128, (dp_ + 1) * 128)
        g_gains[:, cols] = both[0:2, :]
        g_offsets[:, cols] = both[2:4, :]

    across_end(0, 0)
    across_end(0, 1)
    across_end(1, 1)
    direct_end(1, 0)
    drain("grad")
    for ck in range(NCH):
        drain(("part", ck))
    drain("end")
    drain_first()
    drain_second()
    drain_extra()
    drain_plane()


def settle(*refs):
    count = (len(refs) - 1) // 2
    sources, targets, sem = refs[:count], refs[count : 2 * count], refs[-1]
    copies = []
    rows = sources[0].shape[0] // 8
    for k in range(8):
        piece = pl.ds(k * rows, rows)
        copies.append(
            pltpu.make_async_copy(sources[0].at[piece], targets[0].at[piece], sem.at[count + k])
        )
    for n in range(1, count):
        copies.append(pltpu.make_async_copy(sources[n], targets[n], sem.at[n]))
    for copy in copies:
        copy.start()
    for copy in copies:
        copy.wait()


def body(ends_in, ln_gains, ln_biases, qkv_w, qkv_bias, dense_w, up_w, up_bias, down_w, out_bias):
    cosine, sine = rotary_tables()
    vmem = pl.BlockSpec(memory_space=pltpu.VMEM)
    anywhere = pl.BlockSpec(memory_space=pl.ANY)

    def shape(*dims):
        return jax.ShapeDtypeStruct(dims, F32)

    def sems(*dims):
        return pltpu.SemaphoreType.DMA(dims)

    outs = pl.pallas_call(
        kernel,
        out_shape=[
            jax.ShapeDtypeStruct((2 * LEN, D), BF),
            shape(2, D),
            shape(2, D),
            shape(3, 128, 128),
            shape(3, 1, 128),
            shape(128, 128),
            shape(128, 512),
            shape(1, 512),
            shape(512, 128),
            shape(1, D),
        ],
        in_specs=[anywhere] + [vmem] * 11,
        out_specs=[anywhere] + [vmem] * 9,
        scratch_shapes=[
            pltpu.VMEM((128, NALL), BF),
            pltpu.VMEM((8, 256), F32),
            pltpu.VMEM((2, 8, 8, 256), F32),
            pltpu.VMEM((2, 1, 1024), F32),
            pltpu.VMEM((2, 1, 1024), F32),
            pltpu.VMEM((2, D, NALL), BF),
            pltpu.VMEM((LEN, D), BF),
            pltpu.VMEM((2, LEN, D), BF),
            pltpu.VMEM((2, LEN, D), BF),
            pltpu.VMEM((LEN // 8, D), BF),
            pltpu.VMEM((2, LEN, NOUT), BF),
            pltpu.VMEM((2, LEN, 512), BF),
            pltpu.VMEM((2, LEN, 128), BF),
            pltpu.VMEM((2, LEN, 128), BF),
            pltpu.VMEM((2, LEN, 128), BF),
            pltpu.VMEM((2, 128, LEN), BF),
            pltpu.VMEM((2, 128, LEN), BF),
            pltpu.VMEM((2, 10, BQ, 2 * BQ), BF),
            pltpu.VMEM((2, LEN // BQ, 2 * BQ), F32),
            pltpu.VMEM((2, 128, LEN), F32),
            pltpu.VMEM((LEN, 2 * BQ), F32),
            pltpu.VMEM((LEN, 128), BF),
            pltpu.VMEM((LEN, NIN), BF),
            pltpu.VMEM((LEN, 128), F32),
            pltpu.VMEM((LEN, 128), F32),
            pltpu.VMEM((LEN, D), BF),
            pltpu.VMEM((2, LEN // 2, D), BF),
            pltpu.VMEM((2, 3, LEN // 8, D), BF),
            pltpu.VMEM((2, LEN // 8, D), BF),
            pltpu.VMEM((4, 2, 2, 64, NALL), BF),
            pltpu.VMEM((2, 3, 4, 64, NALL), BF),
            pltpu.VMEM((2, 3, 2, 64, NALL), BF),
            pltpu.VMEM((2, 4, 64, NALL), BF),
            pltpu.VMEM((2, 2, 64, NALL), BF),
            pltpu.VMEM((4, 64, NALL), BF),
            pltpu.VMEM((4, 64, NALL), BF),
            pltpu.VMEM((128, NALL), F32),
            pltpu.VMEM((2, 8, 256), F32),
            pltpu.VMEM((16, 8, 256), F32),
            pltpu.VMEM((1, 1024), F32),
            pltpu.VMEM((8, 128), F32),
            pltpu.VMEM((3, 8, 128), F32),
            pltpu.VMEM((16, 8, 128), F32),
            pltpu.SemaphoreType.DMA,
            pltpu.SemaphoreType.DMA,
            pltpu.SemaphoreType.DMA,
            sems(2, 2, 4),
            sems(2, 2, 2, 8),
            sems(2, 2, 4, 3),
            sems(2, 2, 2, 3),
            sems(16),
            sems(2, 8),
            sems(4, NCH, NB),
            sems(4, NCH, NB),
            sems(4, NCH, 3),
            sems(4, NCH, 3),
            sems(2, NCH, 3),
            sems(2, NCH, 3),
            sems(2, NCH, 4),
            sems(2, NCH, 4),
            sems(2, NCH, 4),
            sems(NCH, 8),
            sems(NCH),
            sems(NCH),
            sems(1),
            sems(2),
            sems(2, 3),
            sems(2, 3),
            sems(2, 8),
            sems(16),
            sems(2, 2, 2),
            sems(2, 2, 3),
            sems(2, 2, 3),
            sems(2, 2, 3),
            sems(2, 2, 4),
            sems(2, 4),
            sems(2, 2, 2),
            sems(2, 4),
            sems(3),
            sems(3),
            sems(15),
            sems(16),
        ],
        compiler_params=pltpu.CompilerParams(
            collective_id=0, has_side_effects=True, vmem_limit_bytes=63 * 2**20
        ),
        cost_estimate=pl.CostEstimate(
            flops=22 * 10**9, bytes_accessed=20 * 10**6, transcendentals=4 * 10**6
        ),
    )(
        ends_in[0],
        qkv_w[0],
        dense_w[0],
        up_w[0],
        down_w[0],
        ln_gains[0],
        ln_biases[0],
        jnp.transpose(qkv_bias, (1, 0, 2)),
        up_bias,
        out_bias,
        jnp.asarray(cosine),
        jnp.asarray(sine),
    )
    outs = pl.pallas_call(
        settle,
        out_shape=[jax.ShapeDtypeStruct(out.shape, out.dtype) for out in outs],
        in_specs=[anywhere] * len(outs),
        out_specs=[anywhere] * len(outs),
        scratch_shapes=[sems(len(outs) + 8)],
        cost_estimate=pl.CostEstimate(flops=0, bytes_accessed=10 * 10**6, transcendentals=0),
    )(*outs)
    out, gains, offsets, d_qkv, d_qkv_b, d_dense, d_up, d_up_b, d_down, d_out_b = outs
    return (
        out[None],
        gains[None],
        offsets[None],
        d_qkv[None],
        jnp.transpose(d_qkv_b, (1, 0, 2)),
        d_dense[None],
        d_up[None],
        d_up_b,
        d_down[None],
        d_out_b,
    )


def solution(mesh):
    in_specs = (
        P("section", "dp", None),
        P("section", None, None),
        P("section", None, None),
        P("section", None, "dp", "tensor"),
        P("section", None, "tensor"),
        P("section", "tensor", "dp"),
        P("section", "dp", "tensor"),
        P("section", "tensor"),
        P("section", "tensor", "dp"),
        P("section", None),
    )
    out_specs = (
        P("section", "dp", None),
        P("section", None, None),
        P("section", None, None),
        P("section", None, "dp", "tensor"),
        P("section", None, "tensor"),
        P("section", "tensor", "dp"),
        P("section", "dp", "tensor"),
        P("section", "tensor"),
        P("section", "tensor", "dp"),
        P("section", None),
    )
    return jax.shard_map(body, mesh=mesh, in_specs=in_specs, out_specs=out_specs, check_vma=False)
```

time: 1060 us -> 364 us (0.34)
  waiting for transfers between devices: 601 us -> 0 us
  Pallas kernels: 0 us -> 359 us
  matrix products: 168 us -> 0 us
  other arithmetic: 110 us -> 0 us
  blocking collectives: 94 us -> 0 us
  local copies, waits for them, and re-layouts: 55.6 us -> 0 us
  between operations: 17.2 us -> 1.12 us
    psum x5 -> x0, waiting for transfers between devices: 489 us -> none  [the longest x2 207 us: layer_backward(): lax.psum(d_second.astype(jnp.bfloat16), 'tensor').astype(jnp.float32)]
    pallas_call x0 -> x2, Pallas kernels: none -> 359 us  [the longest x1 206 us: body(): pl.pallas_call(kernel, out_shape=[jax.ShapeDtypeStruct((2 * LEN, D), BF),...]
    dot_general x75 -> x0, matrix products: 162 us -> none  [the longest x3 21.6 us: layer_forward(): jnp.dot(activation, down_w, preferred_element_type=jnp.float32)]
    unnamed x14 -> x0, waiting for transfers between devices: 66.6 us -> none
    all_gather x2 -> x0, blocking collectives: 61.2 us -> none  [the longest x1 34.5 us: fetch_each(): lax.all_gather(shards[0], 'dp', axis=2, tiled=True)]
    reduce_sum x19 -> x0, other arithmetic: 44.7 us -> none  [the longest x3 24.1 us: layer_backward(): jnp.sum(d_first * first_scaled, axis=0)]
    unnamed x457 -> x0, local copies, waits for them, and re-layouts: 36.3 us -> none
    psum x1 -> x0, blocking collectives: 32.8 us -> none  [body(): lax.psum((small_sums[0][None], small_sums[1][None], small_sums[2][None],...]
  transfers between devices with their start and end apart: 15 -> 0, of which waited for: 11 -> 0; matrix products, arithmetic and copies ran while one was open for 12% -> 0% of each run, Pallas kernels for 0% -> 0%
where the time goes in v1:
time: 364 us; the launch traced here: 360 us
  Pallas kernels  359 us (99%)
    pallas_call x1, Pallas kernels, body(): pl.pallas_call(kernel, out_shape=[jax.ShapeDtypeStruct((2 * LEN, D), BF),...  206 us
    pallas_call x1, Pallas kernels, body(): pl.pallas_call(settle, out_shape=[jax.ShapeDtypeStruct(out.shape, out.dty...  153 us

profile of v1, /device:TPU:0, one launch (start us, length us, event | category | flops | bytes accessed | tf_op | source)
XLA Modules:
  0.0 360.3 jit_solution(11418339864546920137)
XLA Ops:
  0.6 206.3 %shard_map.195 = (bf16[2048,1024]{1,0:T(8,128)(2,1)}, f32[2,1024]{1,0:T(2,128)}, f32[2,1024]{1,0:T(2,128)}, f32[3,128,128]{2,1,0:T(8,128)}, f32[3,1,128]{2,1,0:T...) custom-call(bf16[2048,1024]{1,0:T(8,128)(2,1)} %bitcast.16, ...), custom_call_target="tpu_custom_call" | custom-call | flops 22000001024 | bytes 20000000 | tf_op jit(solution)/shard_map/pallas_call | solution.py:1132
  207.0 152.9 %shard_map.196 = (bf16[2048,1024]{1,0:T(8,128)(2,1)}, f32[2,1024]{1,0:T(2,128)}, f32[2,1024]{1,0:T(2,128)}, f32[3,128,128]{2,1,0:T(8,128)}, f32[3,1,128]{2,1,0:T...) custom-call(bf16[2048,1024]{1,0:T(8,128)(2,1)} %get-tuple-element.30, ...), custom_call_target="tpu_custom_call" | custom-call | bytes 10000000 | tf_op jit(solution)/shard_map/pallas_call | solution.py:1252
